TPU v7x, 256 devices: a whole 4x4x8 slice. The times are simulated.
256 devices in a mesh: batch: 4 (over y_hi, core), field: 64 (over z, x, y_lo).
Axes of the slice: x: 4, y: 4 (y_hi: 2, y_lo: 2; y = y_hi * 2 + y_lo), z: 8, core: 2. Of those that a mesh axis runs over, the one named last changes fastest.
Arguments:
- vectors: bfloat16 [4096, 128, 128, 8], P('batch', 'field'), may hold values from -6 to 6
- first_weight: bfloat16 [128, 64, 8, 512], P('field'), may hold values from -0.0234375 to 0.0234375
- second_weight: bfloat16 [512, 256], replicated, may hold values from -0.25 to 0.25
- out_weight: float32 [256], replicated, may hold values from -0.375 to 0.375
- upstream: float32 [4096], P('batch'), may hold values from -6 to 6
Outputs:
- logits: float32 [4096], P('batch')
- grad_vectors: float32 [4096, 128, 128, 8], P('batch', 'field')
- grad_first: float32 [128, 64, 8, 512], P('field', 'batch')
- grad_second: float32 [512, 256], replicated
- grad_out: float32 [256], replicated
All inputs are finite; a program needn't handle non-finite values.
Results may differ from a plain program's by a relative error of at most 0.0067.
Values may be sent and summed in bfloat16 or wider, within the bound.
No kernel may reach another device: no remote copies, remote signals or barrier semaphores. Data moves between devices by JAX's collectives and lax.ppermute only.
A program may use at most 128 MiB of HBM per device.

v0:
```python
import jax
import jax.numpy as jnp
from jax import lax
from jax.sharding import PartitionSpec as P


def silu_slope(value):
    sigmoid_value = jax.nn.sigmoid(value)
    return sigmoid_value * (1.0 + value * (1.0 - sigmoid_value))


def dense_head(hidden, second_weight, out_weight, upstream):
    activated = jax.nn.silu(hidden).astype(jnp.bfloat16)
    second_pre = jnp.dot(activated, second_weight, preferred_element_type=jnp.float32)
    second_act = jax.nn.silu(second_pre)
    logits = jnp.dot(second_act, out_weight, precision=lax.Precision.HIGHEST)
    grad_pre = (upstream[:, None] * out_weight[None, :] * silu_slope(second_pre)).astype(
        jnp.bfloat16
    )
    grad_second = lax.dot_general(
        activated, grad_pre, (((0,), (0,)), ((), ())), preferred_element_type=jnp.float32
    )
    grad_out = lax.dot_general(
        second_act, upstream, (((0,), (0,)), ((), ())), precision=lax.Precision.HIGHEST
    )
    back_hidden = lax.dot_general(
        grad_pre, second_weight, (((1,), (1,)), ((), ())), preferred_element_type=jnp.float32
    )
    grad_hidden = (back_hidden * silu_slope(hidden)).astype(jnp.bfloat16)
    return (logits, grad_second, grad_out, grad_hidden)


def per_device(vectors, first_weight, second_weight, out_weight, upstream):
    row_count, local_fields, field_total, latent = vectors.shape
    hidden_width = first_weight.shape[3]
    half = field_total // 2
    owners = lax.axis_size("field")
    local_half = local_fields // 2
    mine = lax.axis_index("field")
    field_global = mine * local_fields + jnp.arange(local_fields, dtype=jnp.int32)
    slot_index = jnp.arange(half, dtype=jnp.int32)
    odd_field = (field_global % 2 == 1)[:, None]
    lower_slot = slot_index[None, :] <= (field_global // 2)[:, None]
    parity_own = jnp.logical_xor(odd_field, lower_slot)[None, :, :, None]
    invalid = jnp.logical_and(
        jnp.logical_not(odd_field), slot_index[None, :] == (field_global // 2)[:, None]
    )
    valid_mask = jnp.where(invalid, 0.0, 1.0).astype(jnp.float32)[None, :, :, None]
    split_own = vectors.reshape(row_count, local_fields, half, 2, latent)
    own = jnp.where(parity_own, split_own[:, :, :, 1], split_own[:, :, :, 0])
    sender_slot = jnp.arange(local_half, dtype=jnp.int32)[:, None, None]
    target_owner = jnp.arange(owners, dtype=jnp.int32)[None, :, None]
    target_field = jnp.arange(local_fields, dtype=jnp.int32)[None, None, :]
    earlier = mine * local_half + sender_slot <= target_owner * local_half + target_field // 2
    parity_send = jnp.logical_xor(target_field % 2 == 1, earlier)[None, :, :, :, None]
    split_send = vectors.reshape(row_count, local_half, 2, owners, local_fields, latent)
    outgoing = jnp.where(parity_send, split_send[:, :, 1], split_send[:, :, 0])
    outgoing = jnp.transpose(outgoing, (0, 3, 2, 1, 4))
    received = lax.all_to_all(outgoing, "field", split_axis=2, concat_axis=2, tiled=True)
    other = received.reshape(row_count, local_fields, half, latent)
    own_float = own.astype(jnp.float32)
    other_float = other.astype(jnp.float32)
    pairs = (own_float * other_float * valid_mask).astype(jnp.bfloat16)
    weights_flat = first_weight.reshape(-1, hidden_width)
    partial_value = jnp.dot(
        pairs.reshape(row_count, -1), weights_flat, preferred_element_type=jnp.float32
    )
    hidden = lax.psum(partial_value, "field")
    logits, grad_second, grad_out, grad_hidden = dense_head(
        hidden, second_weight, out_weight, upstream
    )
    grad_second, grad_out = lax.psum((grad_second, grad_out), "batch")
    grad_share_first = lax.psum_scatter(
        jnp.einsum("bcmk,bh->mckh", pairs, grad_hidden, preferred_element_type=jnp.float32),
        "batch",
        scatter_dimension=0,
        tiled=True,
    )
    grad_first = jnp.transpose(grad_share_first, (1, 0, 2, 3))
    grad_pairs = lax.dot_general(
        grad_hidden, weights_flat, (((1,), (1,)), ((), ())), preferred_element_type=jnp.float32
    )
    grad_pairs = grad_pairs.reshape(row_count, local_fields, half, latent) * valid_mask
    own_grads = grad_pairs * other_float
    zeros_own = jnp.zeros_like(own_grads)
    own_full = jnp.stack(
        [jnp.where(parity_own, zeros_own, own_grads), jnp.where(parity_own, own_grads, zeros_own)],
        axis=3,
    )
    own_full = own_full.reshape(row_count, local_fields, field_total, latent)
    returning = (grad_pairs * own_float).astype(jnp.bfloat16)
    returning = returning.reshape(row_count, local_fields, owners, local_half, latent)
    arrived = lax.all_to_all(returning, "field", split_axis=2, concat_axis=2, tiled=True)
    arrived = jnp.transpose(arrived.astype(jnp.float32), (0, 3, 2, 1, 4))
    zeros_back = jnp.zeros_like(arrived)
    back_full = jnp.stack(
        [jnp.where(parity_send, zeros_back, arrived), jnp.where(parity_send, arrived, zeros_back)],
        axis=2,
    )
    back_full = back_full.reshape(row_count, local_fields, field_total, latent)
    grad_vectors = own_full + back_full
    return (logits, grad_vectors, grad_first, grad_second, grad_out)


def solution(mesh):
    return jax.shard_map(
        per_device,
        mesh=mesh,
        in_specs=(
            P("batch", "field", None, None),
            P("field", None, None, None),
            P(),
            P(),
            P("batch"),
        ),
        out_specs=(
            P("batch"),
            P("batch", "field", None, None),
            P("field", "batch", None, None),
            P(),
            P(),
        ),
        check_vma=False,
    )
```

profile of v0, /device:TPU:16, one launch (start us, length us, event | category | flops | bytes accessed | tf_op | source)
XLA Modules:
  0.0 817.3 jit_solution(12034932942482532418)
XLA Ops:
  7.2 0.0 copy-start
  7.2 0.1 compare_xor_fusion
  7.3 0.1 copy.42
  7.4 7.5 copy.39
  14.9 3.8 fusion.5
  18.7 12.7 %all-to-all-start = ((bf16[1024,2,64,1,8]{0,4,1,3,2:T(8,128)(2,1)}), bf16[1024,2,64,1,8]{0,4,1,3,2:T(8,128)(2,1)S(1)}, u32[]{:S(2)}, u32[]{:S(2)}) async-start(bf16[1024,2,64,1,8]{0,4,1,3,2:T(8,128)(2,1)} %fusion.5), calls=%async_computation | async-start | bytes 4194304 | tf_op jit(solution)/shard_map/all_to_all | solution.py:59
  31.4 0.0 all-reduce.3.cloned.1.call-start
  31.5 0.1 compare_xor_fusion.1
  31.5 0.1 and_select_fusion
  31.6 4.6 fusion.22
  36.3 46.3 %all-to-all-done = bf16[1024,2,64,1,8]{0,4,1,3,2:T(8,128)(2,1)S(1)} async-done(((bf16[1024,2,64,1,8]{0,4,1,3,2:T(8,128)(2,1)}), bf16[1024,2,64,1,8]{0,4,1,3,2:T(8,128)(2,1)S(1)}, u32[]{:S(2)}, u32[]{:S(2)}) %all-to-all-start) | async-done | bytes 2097184 | tf_op jit(solution)/shard_map/all_to_all | solution.py:59
  82.5 6.0 fusion.2
  88.6 0.0 copy-start.4
  88.6 1.3 copy-done.4
  89.9 0.0 copy-done
  89.9 2.7 convolution_bitcast_fusion
  92.6 0.0 all-reduce.3.cloned.1.call-update
  92.6 0.0 copy-start.11
  92.6 0.0 copy-start.12
  92.6 0.2 reduce-scatter.2.cloned.1.call-start
  92.9 609.2 %all-reduce.3.cloned.1.call-done = f32[1024,512]{1,0:T(8,128)} async-done(((f32[1024,512]{1,0:T(8,128)}), f32[1024,512]{1,0:T(8,128)}) %all-reduce.3.cloned.1.call-update) | async-done | bytes 2097168 | tf_op jit(solution)/shard_map/psum | solution.py:68
  702.1 0.0 copy-start.6
  702.1 2.3 multiply_convert_fusion.1
  704.3 0.0 copy-start.2
  704.4 1.0 copy-done.2
  705.4 0.0 copy-done.10
  705.4 0.4 fusion.25
  705.8 0.0 copy-done.11
  705.8 0.0 copy-done.12
  705.8 0.0 copy-done.6
  705.8 0.0 copy-start.7
  705.8 0.0 copy-start.5
  705.8 1.3 fusion.7
  707.1 0.0 copy-done.7
  707.1 0.0 copy-start.13
  707.1 1.0 copy-done.13
  708.2 0.0 copy-done.5
  708.2 2.6 convolution_bitcast_fusion.1
  710.8 0.0 reduce-scatter.2.cloned.1.call-update
  710.8 12.3 %select_bitcast_fusion.1 = (f32[1024,2,64,1,8]{0,2,4,1,3:T(8,128)}, f32[1024,2,64,1,8]{0,2,4,1,3:T(8,128)}, bf16[1024,2,64,1,8]{0,2,4,1,3:T(8,128)(2,1)S(1)}) fusion(f32[2,64]{1,0:T(2,128)S(1)} %and_select_fusion, pred[2,64]{1,0:T(4,128)(4,1)S(1)} %compare_xor_fusion.1, bf16[1024,2,64,1,8]{0,4,1,3,2:T(8,128)(2,1)S(1)} %all-to-all-done, ...), kind=kOutput, calls=%fused_computation.11 | convolution fusion | flops 1083179008 | bytes 18875008 | tf_op jit(solution)/shard_map/dot_general | solution.py:80
  723.1 2.5 copy.49
  725.6 6.8 all-to-all-start.1
  732.4 0.3 all-reduce.5.cloned.1.call-start
  732.7 4.3 pad_maximum_fusion
  737.0 0.0 copy-start.3
  737.0 0.0 copy-start.8
  737.0 8.3 %copy.48 = f32[1024,2,64,2,8]{0,4,3,2,1:T(8,128)} copy(f32[1024,2,64,2,8]{0,2,4,1,3:T(8,128)S(1)} %pad_maximum_fusion) | data formatting | bytes 16777216 | tf_op jit(solution)/shard_map/stack | solution.py:86
  745.3 0.0 copy-done.3
  745.3 0.0 copy-done.8
  745.3 1.6 fusion.21
  746.9 0.0 all-reduce.5.cloned.1.call-update
  746.9 0.0 copy-start.9
  746.9 2.1 fusion.12
  749.0 8.4 %psum.23 = f32[256]{0:T(256)} all-reduce(f32[256]{0:T(256)S(1)} %bitcast.83), channel_id=1, replica_groups=mesh['batch'=4,'field'=64] {'batch'}, use_global_device_ids=true, to_apply=%region_3.4 | all-reduce | flops 256 | bytes 2048 | tf_op jit(solution)/shard_map/psum | solution.py:72
  757.4 0.0 copy-done.9
  757.4 1.8 fusion.14
  759.3 2.9 all-to-all-done.1
  762.2 0.6 bitcast_select_fusion.1
  762.8 6.4 maximum_add_fusion
  769.2 9.3 %copy.51 = f32[1024,2,128,8]{2,3,1,0:T(8,128)} copy(f32[1024,2,128,8]{0,3,2,1:T(8,128)} %maximum_add_fusion) | data formatting | bytes 16777216
  778.5 2.1 copy.52
  780.6 28.3 %all-reduce.5.cloned.1.call-done = f32[512,256]{1,0:T(8,128)} async-done(((f32[512,256]{1,0:T(8,128)}), f32[512,256]{1,0:T(8,128)}) %all-reduce.5.cloned.1.call-update) | async-done | bytes 524304 | tf_op jit(solution)/shard_map/psum | solution.py:72
  808.9 1.9 copy.82
  810.8 0.0 copy-done.1
  (7 shorter events, 0.0 us)
Async XLA Ops:
  7.2 82.7 %copy-start = (bf16[2,64,8,512]{3,2,1,0:T(8,128)(2,1)S(1)}, bf16[2,64,8,512]{3,2,1,0:T(8,128)(2,1)}, u32[]{:S(2)}) copy-start(bf16[2,64,8,512]{3,2,1,0:T(8,128)(2,1)} %param.6) | copy-start | bytes 3145732
  18.7 63.8 %all-to-all-start = ((bf16[1024,2,64,1,8]{0,4,1,3,2:T(8,128)(2,1)}), bf16[1024,2,64,1,8]{0,4,1,3,2:T(8,128)(2,1)S(1)}, u32[]{:S(2)}, u32[]{:S(2)}) async-start(bf16[1024,2,64,1,8]{0,4,1,3,2:T(8,128)(2,1)} %fusion.5), calls=%async_computation | async-start | bytes 4194304 | tf_op jit(solution)/shard_map/all_to_all | solution.py:59
  31.4 670.7 %all-reduce.3.cloned.1.call-start = ((), (), s32[]{:S(2)}) async-start(), calls=%async_computation.3 | async-start | bytes 4194304 | tf_op jit(solution)/shard_map/psum | solution.py:68
  88.6 1.3 copy-start.4
  92.6 612.8 %copy-start.10 = (bf16[512,256]{1,0:T(8,128)(2,1)S(1)}, bf16[512,256]{1,0:T(8,128)(2,1)}, u32[]{:S(2)}) copy-start(bf16[512,256]{1,0:T(8,128)(2,1)} %param.7) | copy-start | bytes 786436
  92.6 613.2 %copy-start.11 = (f32[1024]{0:T(1024)S(1)}, f32[1024]{0:T(1024)}, u32[]{:S(2)}) copy-start(f32[1024]{0:T(1024)} %param.9) | copy-start | bytes 12292
  92.6 613.2 %copy-start.12 = (f32[256]{0:T(256)S(1)}, f32[256]{0:T(256)}, u32[]{:S(2)}) copy-start(f32[256]{0:T(256)} %param.8) | copy-start | bytes 3076
  92.6 685.9 %reduce-scatter.2.cloned.1.call-start = ((), (), s32[]{:S(2)}) async-start(), calls=%async_computation.4 | async-start | bytes 2621440 | tf_op jit(solution)/shard_map/reduce_scatter | solution.py:73
  702.1 3.8 copy-start.6
  704.3 1.0 copy-start.2
  705.8 1.3 copy-start.7
  705.8 2.3 copy-start.5
  707.1 1.0 copy-start.13
  725.6 36.6 %all-to-all-start.1 = ((bf16[1024,2,64,1,8]{0,4,1,3,2:T(8,128)(2,1)}), bf16[1024,2,64,1,8]{0,4,1,3,2:T(8,128)(2,1)S(1)}, u32[]{:S(2)}, u32[]{:S(2)}) async-start(bf16[1024,2,64,1,8]{0,4,1,3,2:T(8,128)(2,1)} %copy.49), calls=%async_computation.1 | async-start | bytes 4194304 | tf_op jit(solution)/shard_map/all_to_all | solution.py:93
  732.4 76.5 %all-reduce.5.cloned.1.call-start = ((), (), s32[]{:S(2)}) async-start(), calls=%async_computation.5 | async-start | bytes 1048576 | tf_op jit(solution)/shard_map/psum | solution.py:72
  737.0 8.3 %copy-start.3 = (bf16[1024,512]{1,0:T(8,128)(2,1)S(1)}, bf16[1024,512]{1,0:T(8,128)(2,1)}, u32[]{:S(2)}) copy-start(bf16[1024,512]{1,0:T(8,128)(2,1)} %copy-done.2) | copy-start | bytes 3145732
  737.0 8.3 %copy-start.8 = (f32[1024,256]{1,0:T(8,128)S(1)}, f32[1024,256]{1,0:T(8,128)}, u32[]{:S(2)}) copy-start(f32[1024,256]{1,0:T(8,128)} %copy-done.7) | copy-start | bytes 3145732
  746.9 10.6 %copy-start.9 = (f32[1024,256]{1,0:T(8,128)S(1)}, f32[1024,256]{1,0:T(8,128)}, u32[]{:S(2)}) copy-start(f32[1024,256]{1,0:T(8,128)} %copy-done.7) | copy-start | bytes 3145732
  769.2 41.6 %copy-start.1 = (bf16[2,64,8,512]{3,2,1,0:T(8,128)(2,1)S(1)}, bf16[2,64,8,512]{3,2,1,0:T(8,128)(2,1)}, u32[]{:S(2)}) copy-start(bf16[2,64,8,512]{3,2,1,0:T(8,128)(2,1)} %param.6) | copy-start | bytes 3145732
Sparse Core Ops, SparseCore 0:
  92.7 609.2 all-reduce.2
  710.9 47.4 reduce-scatter.1
  761.6 47.2 all-reduce.4
where the time goes:
time: 822 us; the launch traced here: 817 us
  waiting for transfers between devices  687 us (84%)
  local copies, waits for them, and re-layouts  39.7 us (5%)
  matrix products  24.8 us (3%)
  other arithmetic  23.7 us (3%)
  starting transfers between devices  20 us (2%)
  between operations  14 us (2%)
  blocking collectives  8.41 us (1%)
    psum x1, waiting for transfers between devices, per_device(): hidden = lax.psum(partial_value, 'field')  609 us
    all_to_all x1, waiting for transfers between devices, per_device(): lax.all_to_all(outgoing, 'field', split_axis=2, concat_axis=2, tiled=True)  46.3 us
    psum x1, waiting for transfers between devices, per_device(): grad_second, grad_out = lax.psum((grad_second, grad_out), 'batch')  28.3 us
    unnamed x32, local copies, waits for them, and re-layouts  24.2 us
  transfers between devices with their start and end apart: 5, of which 4 were waited for; matrix products, arithmetic and copies ran while one was open for 7% of the time, Pallas kernels for 0%

commit v1 on v0

--- a/solution.py
+++ b/solution.py
@@ -28,6 +28,58 @@
     )
     grad_hidden = (back_hidden * silu_slope(hidden)).astype(jnp.bfloat16)
     return (logits, grad_second, grad_out, grad_hidden)
+
+
+PLANE = 8
+
+
+def inner_groups(owners):
+    return [[base + at for at in range(PLANE)] for base in range(0, owners, PLANE)]
+
+
+def outer_groups(owners):
+    return [[base + at for base in range(0, owners, PLANE)] for at in range(PLANE)]
+
+
+def exchange(blocks, groups):
+    return lax.all_to_all(blocks, "field", 0, 0, axis_index_groups=groups, tiled=True)
+
+
+def field_sum(partial):
+    owners = lax.axis_size("field")
+    inner, outer = inner_groups(owners), outer_groups(owners)
+    depth = owners // PLANE
+    rows, width = partial.shape
+    blocks = partial.astype(jnp.bfloat16).reshape(PLANE, rows // PLANE, width)
+    share = jnp.sum(exchange(blocks, inner).astype(jnp.float32), axis=0)
+    blocks = share.astype(jnp.bfloat16).reshape(depth, rows // owners, width)
+    share = jnp.sum(exchange(blocks, outer).astype(jnp.float32), axis=0)
+    share = share.astype(jnp.bfloat16)
+    copies = jnp.broadcast_to(share[None], (depth,) + share.shape)
+    plane = exchange(copies, outer).reshape(rows // PLANE, width)
+    copies = jnp.broadcast_to(plane[None], (PLANE,) + plane.shape)
+    return exchange(copies, inner).reshape(rows, width).astype(jnp.float32)
+
+
+CORE_PAIRS = [(0, 1), (1, 0), (2, 3), (3, 2)]
+FAR_PAIRS = [(0, 2), (2, 0), (1, 3), (3, 1)]
+
+
+def batch_sum(value):
+    value = value + lax.ppermute(value, "batch", CORE_PAIRS)
+    return value + lax.ppermute(value, "batch", FAR_PAIRS)
+
+
+def batch_scatter(value):
+    place = lax.axis_index("batch")
+    far, core = place // 2, place % 2
+    split = value.reshape((2, 2, value.shape[0] // 4) + value.shape[1:])
+    keep = lax.dynamic_index_in_dim(split, core, 1, keepdims=False)
+    give = lax.dynamic_index_in_dim(split, 1 - core, 1, keepdims=False)
+    split = keep + lax.ppermute(give, "batch", CORE_PAIRS)
+    keep = lax.dynamic_index_in_dim(split, far, 0, keepdims=False)
+    give = lax.dynamic_index_in_dim(split, 1 - far, 0, keepdims=False)
+    return keep + lax.ppermute(give, "batch", FAR_PAIRS)
 
 
 def per_device(vectors, first_weight, second_weight, out_weight, upstream):
@@ -65,16 +117,14 @@
     partial_value = jnp.dot(
         pairs.reshape(row_count, -1), weights_flat, preferred_element_type=jnp.float32
     )
-    hidden = lax.psum(partial_value, "field")
+    hidden = field_sum(partial_value)
     logits, grad_second, grad_out, grad_hidden = dense_head(
         hidden, second_weight, out_weight, upstream
     )
-    grad_second, grad_out = lax.psum((grad_second, grad_out), "batch")
-    grad_share_first = lax.psum_scatter(
-        jnp.einsum("bcmk,bh->mckh", pairs, grad_hidden, preferred_element_type=jnp.float32),
-        "batch",
-        scatter_dimension=0,
-        tiled=True,
+    grad_second = batch_sum(grad_second)
+    grad_out = batch_sum(grad_out)
+    grad_share_first = batch_scatter(
+        jnp.einsum("bcmk,bh->mckh", pairs, grad_hidden, preferred_element_type=jnp.float32)
     )
     grad_first = jnp.transpose(grad_share_first, (1, 0, 2, 3))
     grad_pairs = lax.dot_general(

time: 822 us -> 237 us (0.29)
  waiting for transfers between devices: 687 us -> 67.2 us
  blocking collectives: 8.41 us -> 56.6 us
  between operations: 14 us -> 0.92 us
    psum x2 -> x0, waiting for transfers between devices: 637 us -> none  [the longest x1 609 us: per_device(): hidden = lax.psum(partial_value, 'field')]
    all_to_all x0 -> x4, blocking collectives: none -> 56.6 us  [exchange(): lax.all_to_all(blocks, 'field', 0, 0, axis_index_groups=groups, tiled=True)]
    ppermute x0 -> x6, waiting for transfers between devices: none -> 20.8 us  [the longest x2 20.8 us: batch_sum(): return value + lax.ppermute(value, 'batch', FAR_PAIRS)]
    psum x1 -> x0, blocking collectives: 8.41 us -> none  [per_device(): grad_second, grad_out = lax.psum((grad_second, grad_out), 'batch')]
    unnamed x32 -> x40, local copies, waits for them, and re-layouts: 24.2 us -> 24.5 us
  transfers between devices with their start and end apart: 5 -> 8, of which waited for: 4 -> 2; matrix products, arithmetic and copies ran while one was open for 7% -> 14% of each run, Pallas kernels for 0% -> 0%
where the time goes in v1:
time: 237 us; the launch traced here: 234 us
  waiting for transfers between devices  67.2 us (28%)
  blocking collectives  56.6 us (24%)
  local copies, waits for them, and re-layouts  41.2 us (17%)
  other arithmetic  24.5 us (10%)
  starting transfers between devices  22.6 us (10%)
  matrix products  21.4 us (9%)
    all_to_all x4, blocking collectives, exchange(): lax.all_to_all(blocks, 'field', 0, 0, axis_index_groups=groups, tiled=True)  56.6 us
    all_to_all x1, waiting for transfers between devices, per_device(): lax.all_to_all(outgoing, 'field', split_axis=2, concat_axis=2, tiled=True)  46.4 us
    unnamed x40, local copies, waits for them, and re-layouts  24.5 us
    ppermute x2, waiting for transfers between devices, batch_sum(): return value + lax.ppermute(value, 'batch', FAR_PAIRS)  20.8 us
    all_to_all x1, starting transfers between devices, per_device(): lax.all_to_all(outgoing, 'field', split_axis=2, concat_axis=2, tiled=True)  12.7 us
    dot_general x1, matrix products, per_device(): lax.dot_general(grad_hidden, weights_flat, (((1,), (1,)), ((), ())), pref...  10 us
    another operation x1, local copies, waits for them, and re-layouts, per_device(): jnp.stack([jnp.where(parity_own, zeros_own, own_grads), jnp.where(parity_...  8.25 us
    convert_element_type x1, other arithmetic, per_device(): pairs = (own_float * other_float * valid_mask).astype(jnp.bfloat16)  6.02 us
  transfers between devices with their start and end apart: 8, of which 2 were waited for; matrix products, arithmetic and copies ran while one was open for 14% of the time, Pallas kernels for 0%

profile of v1, /device:TPU:16, one launch (start us, length us, event | category | flops | bytes accessed | tf_op | source)
XLA Modules:
  0.0 234.4 jit_solution(894321057889134935)
XLA Ops:
  0.6 0.0 copy-start
  0.7 0.1 compare_xor_fusion
  0.8 0.1 copy.74
  0.9 7.5 %copy.71 = bf16[1024,2,128,8]{0,3,2,1:T(8,128)(2,1)} copy(bf16[1024,2,128,8]{2,3,1,0:T(8,128)(2,1)} %param.5) | data formatting | bytes 8388608 | tf_op args[0]
  8.3 3.9 %fusion.13 = bf16[1024,2,64,1,8]{0,4,1,3,2:T(8,128)(2,1)} fusion(bf16[1024,1,2,64,2,8]{0,5,4,3,2,1:T(8,128)(2,1)} %bitcast.98, pred[64,2]{1,0:T(8,128)(4,1)S(1)} %copy.74), kind=kLoop, calls=%fused_computation.26 | loop fusion | flops 1048576 | bytes 6291584 | tf_op jit(solution)/shard_map/transpose | solution.py:110
  12.2 12.7 %all-to-all-start = ((bf16[1024,2,64,1,8]{0,4,1,3,2:T(8,128)(2,1)}), bf16[1024,2,64,1,8]{0,4,1,3,2:T(8,128)(2,1)S(1)}, u32[]{:S(2)}, u32[]{:S(2)}) async-start(bf16[1024,2,64,1,8]{0,4,1,3,2:T(8,128)(2,1)} %fusion.13), calls=%async_computation | async-start | bytes 4194304 | tf_op jit(solution)/shard_map/all_to_all | solution.py:111
  24.9 0.1 compare_xor_fusion.1
  25.0 0.1 and_select_fusion
  25.0 4.6 %fusion.32 = (bf16[1024,2,64,1,8]{0,4,3,2,1:T(8,128)(2,1)}, bf16[1024,2,64,1,8]{0,4,3,2,1:T(8,128)(2,1)}) fusion(bf16[1024,2,64,2,8]{0,4,3,2,1:T(8,128)(2,1)} %bitcast.99), kind=kLoop, calls=%fused_computation.69 | loop fusion | bytes 8388608 | tf_op jit(solution)/shard_map/slice | solution.py:102
  29.7 46.4 %all-to-all-done = bf16[1024,2,64,1,8]{0,4,1,3,2:T(8,128)(2,1)S(1)} async-done(((bf16[1024,2,64,1,8]{0,4,1,3,2:T(8,128)(2,1)}), bf16[1024,2,64,1,8]{0,4,1,3,2:T(8,128)(2,1)S(1)}, u32[]{:S(2)}, u32[]{:S(2)}) %all-to-all-start) | async-done | bytes 2097184 | tf_op jit(solution)/shard_map/all_to_all | solution.py:111
  76.0 6.0 %fusion.2 = bf16[1024,2,64,8]{0,2,3,1:T(8,128)(2,1)S(1)} fusion(f32[2,64]{1,0:T(2,128)S(1)} %and_select_fusion, bf16[1024,2,64,1,8]{0,4,1,3,2:T(8,128)(2,1)S(1)} %all-to-all-done, bf16[1024,2,64,1,8]{0,4,3,2,1:T(8,128)(2,1)} %get-tuple-element.34, bf16[1024,2,64,1,8]{0,4,3,2,1:T(8,128)(2,1)} %get-tuple-element.33, pred[2,64]{1,0:T(4,128)(4,1)S(1)} %compare_xor_fusion.1), kind=kLoop, calls=%fused_computation.7 | loop fusion | flops 6291456 | bytes 8389248 | tf_op jit(solution)/shard_map/convert_element_type | solution.py:115
  82.1 1.3 bitcast_convert_fusion
  83.4 0.0 copy-done.9
  83.4 17.2 %all_to_all.30 = bf16[8,128,512]{2,1,0:T(8,128)(2,1)} all-to-all(bf16[8,128,512]{2,1,0:T(8,128)(2,1)S(1)} %bitcast.105), channel_id=1, replica_groups={{0,1,2,3,4,5,6,7},{8,9,10,11,12,13,14,15},{16,17,18,19,20,21,22,23},{24..., dimensions={0} | all-to-all | bytes 2097152 | tf_op jit(solution)/shard_map/all_to_all | solution.py:45
  100.7 1.4 reduce_sum.24
  102.0 13.6 %all_to_all.31 = bf16[8,16,512]{2,1,0:T(8,128)(2,1)S(1)} all-to-all(bf16[8,16,512]{2,1,0:T(8,128)(2,1)S(1)} %bitcast.106), channel_id=1, replica_groups={{0,8,16,24,32,40,48,56},{1,9,17,25,33,41,49,57},{2,10,18,26,34,42,50,58..., dimensions={0} | all-to-all | bytes 262144 | tf_op jit(solution)/shard_map/all_to_all | solution.py:45
  115.7 11.5 %all_to_all.32 = bf16[8,16,512]{2,1,0:T(8,128)(2,1)S(1)} all-to-all(bf16[8,16,512]{2,1,0:T(8,128)(2,1)S(1)} %broadcast_in_dim.77), channel_id=1, replica_groups={{0,8,16,24,32,40,48,56},{1,9,17,25,33,41,49,57},{2,10,18,26,34,42,50,58..., dimensions={0} | all-to-all | bytes 262144 | tf_op jit(solution)/shard_map/all_to_all | solution.py:45
  127.2 0.1 broadcast_in_dim.79
  127.3 0.0 copy-start.13
  127.3 14.3 %all_to_all.33 = bf16[8,128,512]{2,1,0:T(8,128)(2,1)S(1)} all-to-all(bf16[8,128,512]{2,1,0:T(8,128)(2,1)S(1)} %broadcast_in_dim.79), channel_id=1, replica_groups={{0,1,2,3,4,5,6,7},{8,9,10,11,12,13,14,15},{16,17,18,19,20,21,22,23},{24..., dimensions={0} | all-to-all | bytes 2097152 | tf_op jit(solution)/shard_map/all_to_all | solution.py:45
  141.6 0.7 fusion.6
  142.3 0.0 copy-done.13
  142.3 0.0 copy-start.5
  142.3 0.4 fusion.35
  142.7 0.6 copy-done.5
  143.3 1.1 copy-done.10
  144.4 1.3 fusion.15
  145.7 0.3 copy-done.3
  145.9 0.6 copy-done.4
  146.6 10.0 %select_bitcast_fusion.1 = (f32[1024,2,64,1,8]{0,2,4,1,3:T(8,128)}, f32[1024,2,64,1,8]{0,2,4,1,3:T(8,128)}, bf16[1024,2,64,1,8]{0,2,4,1,3:T(8,128)(2,1)S(1)}) fusion(f32[2,64]{1,0:T(2,128)S(1)} %and_select_fusion, pred[2,64]{1,0:T(4,128)(4,1)S(1)} %compare_xor_fusion.1, bf16[1024,2,64,1,8]{0,4,1,3,2:T(8,128)(2,1)S(1)} %all-to-all-done, ...), kind=kOutput, calls=%fused_computation.11 | convolution fusion | flops 1083179008 | bytes 18875008 | tf_op jit(solution)/shard_map/dot_general | solution.py:130
  156.6 2.5 %copy.81 = bf16[1024,2,64,1,8]{0,4,1,3,2:T(8,128)(2,1)} copy(bf16[1024,2,64,1,8]{0,2,4,1,3:T(8,128)(2,1)S(1)} %get-tuple-element.32) | data formatting | bytes 4194304 | tf_op jit(solution)/shard_map/reshape | solution.py:142
  159.1 4.8 %all-to-all-start.5 = ((bf16[1024,2,64,1,8]{0,4,1,3,2:T(8,128)(2,1)}), bf16[1024,2,64,1,8]{0,4,1,3,2:T(8,128)(2,1)S(1)}, u32[]{:S(2)}, u32[]{:S(2)}) async-start(bf16[1024,2,64,1,8]{0,4,1,3,2:T(8,128)(2,1)} %copy.81), calls=%async_computation.5 | async-start | bytes 4194304 | tf_op jit(solution)/shard_map/all_to_all | solution.py:143
  164.0 2.8 %fusion.36 = f32[512,2,64,8]{0,2,3,1:T(8,128)S(1)} fusion(bf16[1024,512,1,1]{1,0,3,2:T(8,128)(2,1)S(1)} %copy-done.17, bf16[1024,2,64,8]{0,2,3,1:T(8,128)(2,1)} %copy-done.9), kind=kOutput, calls=%fused_computation.71 | convolution fusion | flops 1073741824 | bytes 5242880 | tf_op jit(solution)/shard_map/bcmk,bh->mckh/dot_general | solution.py:127
  166.8 0.2 constant_dynamic-slice_fusion.1
  167.0 1.6 copy.120
  168.6 0.0 collective-permute-start
  168.6 1.5 fusion.31
  170.2 0.5 collective-permute-start.2
  170.7 2.2 fusion.22
  172.9 0.0 collective-permute-start.4
  172.9 0.0 collective-permute-done.2
  172.9 1.3 add.148
  174.2 0.7 collective-permute-start.3
  174.9 0.0 collective-permute-done
  174.9 2.1 fusion.16
  176.9 0.8 dynamic-slice_bitcast_fusion
  177.8 2.9 %collective-permute-start.1 = (f32[16,2,8,512]{3,2,1,0:T(8,128)}, f32[16,2,8,512]{3,2,1,0:T(8,128)}, u32[]{:S(2)}, u32[]{:S(2)}) collective-permute-start(f32[16,2,8,512]{3,2,1,0:T(8,128)} %dynamic-slice_bitcast_fusion), channel_id=1, source_target_pairs={{0,128},{128,0},{64,192},{192,64},{1,129},{129,1},{65,193},{193,65... | collective-permute-start | bytes 1572872 | tf_op jit(solution)/shard_map/ppermute | solution.py:82
  180.7 1.7 pad_maximum_fusion
  182.3 0.0 collective-permute-done.4
  182.4 1.0 collective-permute-start.5
  183.3 1.8 fusion.24
  185.2 8.3 %copy.80 = f32[1024,2,64,2,8]{0,4,3,2,1:T(8,128)} copy(f32[1024,2,64,2,8]{0,2,4,1,3:T(8,128)S(1)} %pad_maximum_fusion) | data formatting | bytes 16777216 | tf_op jit(solution)/shard_map/stack | solution.py:136
  193.4 20.8 %collective-permute-done.5 = f32[256]{0:T(256)S(1)} collective-permute-done((f32[256]{0:T(256)S(1)}, f32[256]{0:T(256)S(1)}, u32[]{:S(2)}, u32[]{:S(2)}) %collective-permute-start.5) | collective-permute-done | bytes 1056 | tf_op jit(solution)/shard_map/ppermute | solution.py:70
  214.2 0.6 add.151
  214.7 0.0 collective-permute-done.3
  214.7 0.9 add.149
  215.6 0.0 collective-permute-done.1
  215.6 1.1 fusion.21
  216.7 0.8 copy.86
  217.6 0.0 all-to-all-done.5
  217.6 0.6 bitcast_select_fusion.1
  218.2 2.8 %copy-done.2 = f32[1024,2,64,2,8]{0,4,3,2,1:T(8,128)S(1)} copy-done((f32[1024,2,64,2,8]{0,4,3,2,1:T(8,128)S(1)}, f32[1024,2,64,2,8]{0,4,3,2,1:T(8,128)}, u32[]{:S(2)}) %copy-start.2) | copy-done | bytes 8388632
  221.0 4.2 %maximum_add_fusion = f32[1024,2,128,8]{0,3,2,1:T(8,128)} fusion(f32[1024,2,128,8]{0,3,2,1:T(8,128)S(1)} %bitcast.100, f32[1024,1,128,8]{0,3,2,1:T(8,128)S(1)} %bitcast.102, f32[1024,1,128,8]{0,3,2,1:T(8,128)S(1)} %bitcast.101), kind=kLoop, calls=%fused_computation.1 | loop fusion | flops 4194304 | bytes 25165824 | tf_op jit(solution)/shard_map/add | solution.py:151
  225.2 9.3 %copy.85 = f32[1024,2,128,8]{2,3,1,0:T(8,128)} copy(f32[1024,2,128,8]{0,3,2,1:T(8,128)} %maximum_add_fusion) | data formatting | bytes 16777216
  (33 shorter events, 0.1 us)
Async XLA Ops:
  0.6 81.4 %copy-start = (bf16[2,64,8,512]{3,2,1,0:T(8,128)(2,1)S(1)}, bf16[2,64,8,512]{3,2,1,0:T(8,128)(2,1)}, u32[]{:S(2)}) copy-start(bf16[2,64,8,512]{3,2,1,0:T(8,128)(2,1)} %param.6) | copy-start | bytes 3145732
  12.2 63.8 %all-to-all-start = ((bf16[1024,2,64,1,8]{0,4,1,3,2:T(8,128)(2,1)}), bf16[1024,2,64,1,8]{0,4,1,3,2:T(8,128)(2,1)S(1)}, u32[]{:S(2)}, u32[]{:S(2)}) async-start(bf16[1024,2,64,1,8]{0,4,1,3,2:T(8,128)(2,1)} %fusion.13), calls=%async_computation | async-start | bytes 4194304 | tf_op jit(solution)/shard_map/all_to_all | solution.py:111
  82.0 1.4 copy-start.9
  127.3 15.0 %copy-start.13 = (bf16[512,256]{1,0:T(8,128)(2,1)S(1)}, bf16[512,256]{1,0:T(8,128)(2,1)}, u32[]{:S(2)}) copy-start(bf16[512,256]{1,0:T(8,128)(2,1)} %param.7) | copy-start | bytes 786436
  141.6 2.7 %copy-start.14 = (f32[1024]{0:T(1024)S(1)}, f32[1024]{0:T(1024)}, u32[]{:S(2)}) copy-start(f32[1024]{0:T(1024)} %param.9) | copy-start | bytes 12292
  141.6 2.7 %copy-start.15 = (f32[256]{0:T(256)S(1)}, f32[256]{0:T(256)}, u32[]{:S(2)}) copy-start(f32[256]{0:T(256)} %param.8) | copy-start | bytes 3076
  142.3 1.0 copy-start.5
  143.3 1.1 copy-start.10
  144.3 1.6 copy-start.3
  144.3 2.2 copy-start.4
  146.6 10.0 %copy-start.16 = (bf16[1024,512,1,1]{1,0,3,2:T(8,128)(2,1)}, bf16[1024,512,1,1]{1,0,3,2:T(8,128)(2,1)S(1)}, u32[]{:S(2)}) copy-start(bf16[1024,512,1,1]{1,0,3,2:T(8,128)(2,1)S(1)} %fusion.15) | copy-start | bytes 3145732
  159.1 4.9 %copy-start.17 = (bf16[1024,512,1,1]{1,0,3,2:T(8,128)(2,1)S(1)}, bf16[1024,512,1,1]{1,0,3,2:T(8,128)(2,1)}, u32[]{:S(2)}) copy-start(bf16[1024,512,1,1]{1,0,3,2:T(8,128)(2,1)} %copy-done.16) | copy-start | bytes 3145732
  159.1 58.5 %all-to-all-start.5 = ((bf16[1024,2,64,1,8]{0,4,1,3,2:T(8,128)(2,1)}), bf16[1024,2,64,1,8]{0,4,1,3,2:T(8,128)(2,1)S(1)}, u32[]{:S(2)}, u32[]{:S(2)}) async-start(bf16[1024,2,64,1,8]{0,4,1,3,2:T(8,128)(2,1)} %copy.81), calls=%async_computation.5 | async-start | bytes 4194304 | tf_op jit(solution)/shard_map/all_to_all | solution.py:143
  167.0 1.6 copy-start.6
  167.0 1.6 copy-start.11
  168.6 6.3 %collective-permute-start = (f32[2,16,2,8,512]{4,3,2,1,0:T(8,128)}, f32[2,16,2,8,512]{4,3,2,1,0:T(8,128)}, u32[]{:S(2)}, u32[]{:S(2)}) collective-permute-start(f32[2,16,2,8,512]{4,3,2,1,0:T(8,128)} %bitcast.97), channel_id=1, source_target_pairs={{0,64},{64,0},{128,192},{192,128},{1,65},{65,1},{129,193},{193,129... | collective-permute-start | bytes 3145736 | tf_op jit(solution)/shard_map/ppermute | solution.py:79
  170.2 2.7 %collective-permute-start.2 = (f32[512,256]{1,0:T(8,128)}, f32[512,256]{1,0:T(8,128)}, u32[]{:S(2)}, u32[]{:S(2)}) collective-permute-start(f32[512,256]{1,0:T(8,128)} %fusion.31), channel_id=1, source_target_pairs={{0,64},{64,0},{128,192},{192,128},{1,65},{65,1},{129,193},{193,129... | collective-permute-start | bytes 1572872 | tf_op jit(solution)/shard_map/ppermute | solution.py:69
  170.7 10.0 %copy-start.8 = (f32[1024,2,64,1,8]{0,2,4,1,3:T(8,128)S(1)}, f32[1024,2,64,1,8]{0,2,4,1,3:T(8,128)}, u32[]{:S(2)}) copy-start(f32[1024,2,64,1,8]{0,2,4,1,3:T(8,128)} %get-tuple-element.31) | copy-start | bytes 12582916
  172.9 9.5 %collective-permute-start.4 = (f32[256]{0:T(256)S(1)}, f32[256]{0:T(256)S(1)}, u32[]{:S(2)}, u32[]{:S(2)}) collective-permute-start(f32[256]{0:T(256)S(1)} %bitcast.108), channel_id=1, source_target_pairs={{0,64},{64,0},{128,192},{192,128},{1,65},{65,1},{129,193},{193,129... | collective-permute-start | bytes 3080 | tf_op jit(solution)/shard_map/ppermute | solution.py:69
  174.2 40.6 %collective-permute-start.3 = (f32[512,256]{1,0:T(8,128)S(1)}, f32[512,256]{1,0:T(8,128)S(1)}, u32[]{:S(2)}, u32[]{:S(2)}) collective-permute-start(f32[512,256]{1,0:T(8,128)S(1)} %add.148), channel_id=1, source_target_pairs={{0,128},{128,0},{64,192},{192,64},{1,129},{129,1},{65,193},{193,65... | collective-permute-start | bytes 1572872 | tf_op jit(solution)/shard_map/ppermute | solution.py:70
  174.9 5.8 %copy-start.7 = (f32[1024,2,64,1,8]{0,2,4,1,3:T(8,128)S(1)}, f32[1024,2,64,1,8]{0,2,4,1,3:T(8,128)}, u32[]{:S(2)}) copy-start(f32[1024,2,64,1,8]{0,2,4,1,3:T(8,128)} %get-tuple-element.30) | copy-start | bytes 12582916
  177.8 37.8 %collective-permute-start.1 = (f32[16,2,8,512]{3,2,1,0:T(8,128)}, f32[16,2,8,512]{3,2,1,0:T(8,128)}, u32[]{:S(2)}, u32[]{:S(2)}) collective-permute-start(f32[16,2,8,512]{3,2,1,0:T(8,128)} %dynamic-slice_bitcast_fusion), channel_id=1, source_target_pairs={{0,128},{128,0},{64,192},{192,64},{1,129},{129,1},{65,193},{193,65... | collective-permute-start | bytes 1572872 | tf_op jit(solution)/shard_map/ppermute | solution.py:82
  180.7 2.7 %copy-start.12 = (f32[1024,256]{1,0:T(8,128)S(1)}, f32[1024,256]{1,0:T(8,128)}, u32[]{:S(2)}) copy-start(f32[1024,256]{1,0:T(8,128)} %copy-done.10) | copy-start | bytes 3145732
  182.4 31.8 %collective-permute-start.5 = (f32[256]{0:T(256)S(1)}, f32[256]{0:T(256)S(1)}, u32[]{:S(2)}, u32[]{:S(2)}) collective-permute-start(f32[256]{0:T(256)S(1)} %add.150), channel_id=1, source_target_pairs={{0,128},{128,0},{64,192},{192,64},{1,129},{129,1},{65,193},{193,65... | collective-permute-start | bytes 3080 | tf_op jit(solution)/shard_map/ppermute | solution.py:70
  217.6 3.4 %copy-start.2 = (f32[1024,2,64,2,8]{0,4,3,2,1:T(8,128)S(1)}, f32[1024,2,64,2,8]{0,4,3,2,1:T(8,128)}, u32[]{:S(2)}) copy-start(f32[1024,2,64,2,8]{0,4,3,2,1:T(8,128)} %copy.80) | copy-start | bytes 25165828
  225.2 9.3 %copy-start.1 = (bf16[2,64,8,512]{3,2,1,0:T(8,128)(2,1)S(1)}, bf16[2,64,8,512]{3,2,1,0:T(8,128)(2,1)}, u32[]{:S(2)}) copy-start(bf16[2,64,8,512]{3,2,1,0:T(8,128)(2,1)} %param.6) | copy-start | bytes 3145732
